TPU v7x, 512 devices: a whole 4x4x16 slice. The times are simulated.
512 devices in a mesh: section: 64 (over z, y_lo, core), tensor: 8 (over x, y_hi).
Axes of the slice: x: 4, y: 4 (y_hi: 2, y_lo: 2; y = y_hi * 2 + y_lo), z: 16, core: 2. Of those that a mesh axis runs over, the one named last changes fastest.
Arguments:
- queries: bfloat16 [24576, 5120], P('section', 'tensor'), may hold values from -6 to 6, as said below
- keys: bfloat16 [24576, 5120], P('section', 'tensor'), may hold values from -6 to 6, as said below
- values: bfloat16 [24576, 5120], P('section', 'tensor'), may hold values from -12 to 12
- q_gain: float32 [5120], P('tensor'), may hold values from 1 to 2.5
- k_gain: float32 [5120], P('tensor'), may hold values from 1 to 2.5
- frame_offset: int32 [64], P('section'), may hold values from 0 to 255, as said below
- noise_level: int32 [64], P('section'), may hold values from 0 to 127, as said below
- gate_table: float32 [128, 5120], P(None, 'tensor'), may hold values from -6 to 6
- out_weight: bfloat16 [5120, 5120], P('tensor', 'section'), may hold values from -0.078125 to 0.078125
- latent: bfloat16 [24576, 5120], P('section', 'tensor'), may hold values from -6 to 6
- fresh: bfloat16 [384, 5120], P(None, 'tensor'), may hold values from -6 to 6
Outputs:
- queue_next: bfloat16 [24576, 5120], P('section', 'tensor')
Inputs may be any that keep to these rules, and one draw needn't show every extreme that they name: `queries`: entries are real values; rows are not normalized. `keys`: entries are real values; rows are not normalized. `frame_offset`: frame 0 has offset 0, the last frame 4 * 64 - 1, and offsets rise by 1 to 7 from each frame to the next. `noise_level`: frame 0 has level 0, the last frame 128 - 1, and levels rise by 1 to 3 from each frame to the next.
All inputs are finite; a program needn't handle non-finite values.
Results may differ from a plain program's by a relative error of at most 0.013.
Values may be sent and summed in bfloat16 or wider, within the bound.
A program may use at most 64 MiB of HBM per device.

v0:
```python
import math

import jax
import jax.numpy as jnp
from jax import lax
from jax.sharding import PartitionSpec as P

D = 5120
HD = 128


EPSILON = 1e-06


def with_halo(block, sides, width):
    for axis, dim in sides:
        count = lax.axis_size(axis)
        forward = [(i, i + 1) for i in range(count - 1)]
        backward = [(target, source) for source, target in forward]
        low = lax.ppermute(
            lax.slice_in_dim(block, block.shape[dim] - width, None, axis=dim), axis, forward
        )
        high = lax.ppermute(lax.slice_in_dim(block, 0, width, axis=dim), axis, backward)
        block = jnp.concatenate([low, block, high], axis=dim)
    return block


def from_behind(value, axis, by):
    length = lax.axis_size(axis)
    pairs = [(i, i + by) for i in range(length) if 0 <= i + by < length]
    return lax.ppermute(value, axis, pairs)


def rotate(inputs, offsets):
    half_width = HD // 2
    pair_index = jnp.arange(half_width, dtype=jnp.float32)
    pair_rate = jnp.exp(pair_index * (-math.log(10000.0) / half_width))
    angles = offsets.astype(jnp.float32)[:, None, None] * pair_rate
    row_count = inputs.shape[0]
    by_head = inputs.reshape(row_count, -1, HD)
    leading = by_head[..., :half_width]
    trailing = by_head[..., half_width:]
    cosines = jnp.cos(angles)
    sine_part = jnp.sin(angles)
    turned = jnp.concatenate(
        [leading * cosines - trailing * sine_part, leading * sine_part + trailing * cosines],
        axis=-1,
    )
    return turned.reshape(row_count, -1)


def attend_local(q_block, k_block, v_block, usable):
    tokens = q_block.shape[0]
    q_heads = q_block.reshape(tokens, -1, HD)
    k_heads = k_block.reshape(k_block.shape[0], -1, HD)
    v_heads = v_block.reshape(v_block.shape[0], -1, HD)
    scores = jnp.einsum("qhd,khd->hqk", q_heads, k_heads, preferred_element_type=jnp.float32) * (
        1.0 / math.sqrt(HD)
    )
    scores = jnp.where(usable[None, None, :], scores, -jnp.inf)
    highest = jnp.max(scores, axis=-1, keepdims=True)
    raised = jnp.exp(scores - highest)
    weights = (raised / jnp.sum(raised, axis=-1, keepdims=True)).astype(jnp.bfloat16)
    mixed = jnp.einsum("hqk,khd->qhd", weights, v_heads, preferred_element_type=jnp.float32)
    return mixed.astype(jnp.bfloat16).reshape(tokens, -1)


def body(
    queries,
    keys,
    values,
    q_gain,
    k_gain,
    frame_offset,
    noise_level,
    gate_table,
    out_weight,
    latent,
    fresh,
):
    tokens = queries.shape[0]
    position = lax.axis_index("section")
    length = lax.axis_size("section")
    q_wide = queries.astype(jnp.float32)
    k_wide = keys.astype(jnp.float32)
    q_total, k_total = lax.psum(
        (jnp.sum(q_wide * q_wide, axis=-1), jnp.sum(k_wide * k_wide, axis=-1)), "tensor"
    )
    row_offsets = jnp.broadcast_to(frame_offset, (tokens,))
    q_normed = rotate(
        q_wide * lax.rsqrt(q_total / D + EPSILON)[:, None] * q_gain, row_offsets
    ).astype(jnp.bfloat16)
    k_normed = rotate(
        k_wide * lax.rsqrt(k_total / D + EPSILON)[:, None] * k_gain, row_offsets
    ).astype(jnp.bfloat16)
    stacked = jnp.stack([k_normed, values])
    padded = with_halo(stacked, (("section", 1),), tokens)
    block_of = jnp.arange(3 * tokens, dtype=jnp.int32) // tokens
    usable = ((block_of > 0) | (position > 0)) & ((block_of < 2) | (position < length - 1))
    mixed = attend_local(q_normed, padded[0], padded[1], usable)
    source_level = noise_level[0]
    terms = jnp.dot(
        mixed,
        lax.all_gather(out_weight, "section", axis=1, tiled=True),
        preferred_element_type=jnp.float32,
    )
    projected = lax.psum_scatter(
        terms.astype(jnp.bfloat16), "tensor", scatter_dimension=1, tiled=True
    ).astype(jnp.float32)
    gate_row = lax.dynamic_index_in_dim(gate_table, source_level, 0, keepdims=False)
    updated = (latent.astype(jnp.float32) + gate_row * projected).astype(jnp.bfloat16)
    shifted = from_behind(updated, "section", 1)
    return jnp.where(position == 0, fresh, shifted)


def solution(mesh):
    in_specs = (
        P("section", "tensor"),
        P("section", "tensor"),
        P("section", "tensor"),
        P("tensor"),
        P("tensor"),
        P("section"),
        P("section"),
        P(None, "tensor"),
        P("tensor", "section"),
        P("section", "tensor"),
        P(None, "tensor"),
    )
    out_specs = P("section", "tensor")
    return jax.shard_map(body, mesh=mesh, in_specs=in_specs, out_specs=out_specs, check_vma=False)
```

profile of v0, /device:TPU:128, one launch (start us, length us, event | category | flops | bytes accessed | tf_op | source)
XLA Modules:
  0.0 274.5 jit_solution(13286961518657783253)
XLA Ops:
  6.5 0.0 copy-start
  6.5 0.0 copy-start.4
  6.5 0.0 all-gather.2.cloned.1.call-start
  6.5 0.7 all-gather.2.cloned.1.call-update
  7.3 0.0 reduce-scatter.4.cloned.1.call-start
  7.3 1.3 copy.27
  8.6 1.3 copy.22
  9.9 0.1 fusion.11
  10.0 0.1 fusion.9
  10.2 24.3 %all-reduce = (f32[384]{0:T(512)S(1)}, f32[384]{0:T(512)S(1)}) all-reduce(f32[384]{0:T(512)S(1)} %fusion.9, f32[384]{0:T(512)S(1)} %fusion.11), channel_id=1, replica_groups=mesh['section'=64,'tensor'=8] {'tensor'}, use_global_device_ids=true, to_apply=%region_1.0 | all-reduce | flops 768 | bytes 6144 | tf_op jit(solution)/shard_map/psum | solution.py:86
  34.5 0.8 fusion.10
  35.4 0.1 fusion.26
  35.5 0.3 copy.34
  35.8 0.3 copy.35
  36.1 0.0 copy-done.4
  36.2 0.2 fusion.12
  36.3 0.1 fusion.25
  36.4 1.3 copy.36
  37.7 0.0 copy-start.1
  37.7 1.3 copy.37
  39.7 3.0 %subtract_convert_fusion = (bf16[384,5,64]{2,0,1:T(8,128)(2,1)}, bf16[384,5,64]{2,0,1:T(8,128)(2,1)}, bf16[384,5,64]{2,0,1:T(8,128)(2,1)S(1)}, bf16[384,5,64]{2,0,1:T(8,128)(2,1)S(1)}) fusion(f32[384,5,64]{2,0,1:T(8,128)} %copy.37, f32[384,5,64]{2,0,1:T(8,128)} %copy.36, f32[64]{0:T(128)S(1)} %get-tuple-element.21, f32[64]{0:T(128)S(1)} %get-tuple-element.22, ...), kind=kLoop, calls=%fused_computation.24 | loop fusion | flops 1966080 | bytes 2949632 | tf_op jit(solution)/shard_map/convert
  42.8 0.3 pad_maximum_fusion.2
  43.1 0.3 copy.25
  43.3 0.0 copy-done.1
  43.3 0.3 copy.26
  43.6 0.1 pad_maximum_fusion.1
  43.7 1.9 collective-permute-start
  45.6 5.9 %collective-permute-start.1 = (bf16[2,384,640]{1,2,0:T(8,128)(2,1)S(1)}, bf16[2,384,640]{1,2,0:T(8,128)(2,1)}, u32[]{:S(2)}, u32[]{:S(2)}) collective-permute-start(bf16[2,384,640]{1,2,0:T(8,128)(2,1)S(1)} %pad_maximum_fusion.1), channel_id=1, source_target_pairs={{8,0},{16,8},{24,16},{32,24},{40,32},{48,40},{56,48},{64,56},{72,6... | collective-permute-start | bytes 2949128 | tf_op jit(solution)/shard_map/ppermute | solution.py:23
  51.6 15.0 %collective-permute-done = bf16[2,384,640]{1,2,0:T(8,128)(2,1)S(1)} collective-permute-done((bf16[2,384,640]{1,2,0:T(8,128)(2,1)S(1)}, bf16[2,384,640]{1,2,0:T(8,128)(2,1)S(1)}, u32[]{:S(2)}, u32[]{:S(2)}) %collective-permute-start) | collective-permute-done | bytes 983072 | tf_op jit(solution)/shard_map/ppermute | solution.py:20
  66.6 1.6 collective-permute-done.1
  68.2 1.3 pad_maximum_fusion
  69.5 0.2 fusion.24
  69.8 4.1 %fusion.27 = f32[5,384]{1,0:T(8,128)S(1)} fusion(pred[1152]{0:T(1024)(128)(4,1)S(1)} %or_and_fusion, bf16[1152,5,128]{0,2,1:T(8,128)(2,1)S(1)} %bitcast.28, bf16[384,5,64]{2,0,1:T(8,128)(2,1)} %get-tuple-element.10, bf16[384,5,64]{2,0,1:T(8,128)(2,1)} %get-tuple-element.9), kind=kOutput, calls=%fused_computation.51 | convolution fusion | flops 576062592 | bytes 1974912 | tf_op jit(solution)/shard_map/sub | solution.py:62
  73.9 6.1 %fusion.8 = bf16[5,128,384]{2,1,0:T(8,128)(2,1)} fusion(bf16[1152,5,128]{0,2,1:T(8,128)(2,1)S(1)} %bitcast.30, f32[5,384]{1,0:T(8,128)S(1)} %fusion.27, pred[1152]{0:T(1024)(128)(4,1)S(1)} %or_and_fusion, bf16[1152,5,128]{0,2,1:T(8,128)(2,1)S(1)} %bitcast.29, bf16[384,5,64]{2,0,1:T(8,128)(2,1)} %get-tuple-element.10, bf16[384,5,64]{2,0,1:T(8,128)(2,1)} %get-tuple-element.9), kind=kOutput, calls=%fused_computation.12 | convolution fusion | flops 1144753152 | bytes 3940992 | tf_op jit(solution)/shard_map/hqk,khd->qhd/dot_general | solution.py:64
  80.0 59.5 %all-gather.2.cloned.1.call-done = bf16[640,5120]{0,1:T(8,128)(2,1)} async-done(((bf16[640,80]{0,1:T(8,128)(2,1)}), bf16[640,5120]{0,1:T(8,128)(2,1)}) %all-gather.2.cloned.1.call-update) | async-done | bytes 6553616 | tf_op jit(solution)/shard_map/all_gather | solution.py:104
  139.5 8.3 %convolution_convert_fusion = bf16[384,5120]{1,0:T(8,128)(2,1)} fusion(bf16[384,640]{0,1:T(8,128)(2,1)} %bitcast.32, bf16[640,5120]{0,1:T(8,128)(2,1)} %all-gather.2.cloned.1.call-done), kind=kOutput, calls=%fused_computation.5 | convolution fusion | flops 2518548480 | bytes 10977280 | tf_op jit(solution)/shard_map/dot_general | solution.py:102
  147.8 0.0 copy-start.2
  147.8 6.3 %copy.32 = bf16[384,5120]{0,1:T(8,128)(2,1)} copy(bf16[384,5120]{1,0:T(8,128)(2,1)} %convolution_convert_fusion) | data formatting | bytes 7864320
  154.1 0.0 reduce-scatter.4.cloned.1.call-update
  154.8 0.0 copy-done
  154.8 98.3 %reduce-scatter.4.cloned.1.call-done = bf16[640,384]{1,0:T(8,128)(2,1)} async-done(((bf16[5120,384]{1,0:T(8,128)(2,1)}), bf16[640,384]{1,0:T(8,128)(2,1)}) %reduce-scatter.4.cloned.1.call-update) | async-done | bytes 491536
  253.1 1.3 copy.33
  254.4 0.0 copy-done.2
  254.4 0.2 add_convert_fusion
  254.6 1.9 collective-permute-start.2
  256.5 10.3 %collective-permute-done.2 = bf16[384,640]{1,0:T(8,128)(2,1)S(1)} collective-permute-done((bf16[384,640]{1,0:T(8,128)(2,1)S(1)}, bf16[384,640]{1,0:T(8,128)(2,1)S(1)}, u32[]{:S(2)}, u32[]{:S(2)}) %collective-permute-start.2) | collective-permute-done | bytes 491552 | tf_op jit(solution)/shard_map/ppermute | solution.py:31
  266.8 0.0 copy-done.3
  266.8 0.8 broadcast_select_fusion
  (5 shorter events, 0.1 us)
Async XLA Ops:
  6.5 148.2 %copy-start = (f32[128,640]{1,0:T(8,128)S(1)}, f32[128,640]{1,0:T(8,128)}, u32[]{:S(2)}) copy-start(f32[128,640]{1,0:T(8,128)} %param.18) | copy-start | bytes 983044
  6.5 29.6 %copy-start.4 = (f32[640]{0:T(1024)S(1)}, f32[640]{0:T(1024)}, u32[]{:S(2)}) copy-start(f32[640]{0:T(1024)} %param.14) | copy-start | bytes 7684
  6.5 133.0 %all-gather.2.cloned.1.call-start = ((), (), s32[]{:S(2)}) async-start(), calls=%async_computation.1 | async-start | bytes 6656000 | tf_op jit(solution)/shard_map/all_gather | solution.py:104
  7.3 245.9 %reduce-scatter.4.cloned.1.call-start = ((), (), s32[]{:S(2)}) async-start(), calls=%async_computation.2 | async-start | bytes 4423680
  37.7 5.6 %copy-start.1 = (bf16[384,640]{1,0:T(8,128)(2,1)S(1)}, bf16[384,640]{1,0:T(8,128)(2,1)}, u32[]{:S(2)}) copy-start(bf16[384,640]{1,0:T(8,128)(2,1)} %param.13) | copy-start | bytes 1474564
  43.7 22.9 %collective-permute-start = (bf16[2,384,640]{1,2,0:T(8,128)(2,1)S(1)}, bf16[2,384,640]{1,2,0:T(8,128)(2,1)S(1)}, u32[]{:S(2)}, u32[]{:S(2)}) collective-permute-start(bf16[2,384,640]{1,2,0:T(8,128)(2,1)S(1)} %pad_maximum_fusion.1), channel_id=1, source_target_pairs={{0,8},{8,16},{16,24},{24,32},{32,40},{40,48},{48,56},{56,64},{64,7... | collective-permute-start | bytes 2949128 | tf_op jit(solution)/shard_map/ppermute | solution.py:20
  45.6 22.6 %collective-permute-start.1 = (bf16[2,384,640]{1,2,0:T(8,128)(2,1)S(1)}, bf16[2,384,640]{1,2,0:T(8,128)(2,1)}, u32[]{:S(2)}, u32[]{:S(2)}) collective-permute-start(bf16[2,384,640]{1,2,0:T(8,128)(2,1)S(1)} %pad_maximum_fusion.1), channel_id=1, source_target_pairs={{8,0},{16,8},{24,16},{32,24},{40,32},{48,40},{56,48},{64,56},{72,6... | collective-permute-start | bytes 2949128 | tf_op jit(solution)/shard_map/ppermute | solution.py:23
  147.8 106.7 %copy-start.2 = (bf16[384,640]{1,0:T(8,128)(2,1)S(1)}, bf16[384,640]{1,0:T(8,128)(2,1)}, u32[]{:S(2)}) copy-start(bf16[384,640]{1,0:T(8,128)(2,1)} %param.20) | copy-start | bytes 1474564
  147.8 119.1 %copy-start.3 = (bf16[384,640]{1,0:T(8,128)(2,1)S(1)}, bf16[384,640]{1,0:T(8,128)(2,1)}, u32[]{:S(2)}) copy-start(bf16[384,640]{1,0:T(8,128)(2,1)} %param.21) | copy-start | bytes 1474564
  254.6 12.3 %collective-permute-start.2 = (bf16[384,640]{1,0:T(8,128)(2,1)S(1)}, bf16[384,640]{1,0:T(8,128)(2,1)S(1)}, u32[]{:S(2)}, u32[]{:S(2)}) collective-permute-start(bf16[384,640]{1,0:T(8,128)(2,1)S(1)} %add_convert_fusion), channel_id=1, source_target_pairs={{0,8},{8,16},{16,24},{24,32},{32,40},{40,48},{48,56},{56,64},{64,7... | collective-permute-start | bytes 1474568 | tf_op jit(solution)/shard_map/ppermute | solution.py:31
Sparse Core Ops, SparseCore 0:
  9.5 129.9 all-gather.1
  154.3 98.8 reduce-scatter.3
where the time goes:
time: 275 us
  waiting for transfers between devices  185 us (67%)
  blocking collectives  24.3 us (9%)
  matrix products  18.5 us (7%)
  between operations  14.9 us (5%)
  local copies, waits for them, and re-layouts  14.5 us (5%)
  starting transfers between devices  9.81 us (4%)
  other arithmetic  7.1 us (3%)
    unnamed x3, waiting for transfers between devices  99 us
    all_gather x1, waiting for transfers between devices, body(): lax.all_gather(out_weight, 'section', axis=1, tiled=True)  59.5 us
    psum x1, blocking collectives, body(): lax.psum((jnp.sum(q_wide * q_wide, axis=-1), jnp.sum(k_wide * k_wide, axi...  24.3 us
    ppermute x1, waiting for transfers between devices, with_halo(): lax.ppermute(lax.slice_in_dim(block, block.shape[dim] - width, None, axis...  15 us
    unnamed x19, local copies, waits for them, and re-layouts  13.8 us
    ppermute x1, waiting for transfers between devices, from_behind(): return lax.ppermute(value, axis, pairs)  10.3 us
    dot_general x1, matrix products, body(): jnp.dot(mixed, lax.all_gather(out_weight, 'section', axis=1, tiled=True),...  8.26 us
    dot_general x1, matrix products, attend_local(): jnp.einsum('hqk,khd->qhd', weights, v_heads, preferred_element_type=jnp.f...  6.13 us
  transfers between devices with their start and end apart: 5, of which 5 were waited for; matrix products, arithmetic and copies ran while one was open for 8% of the time, Pallas kernels for 0%

commit v1 on v0

v1 whole, which is shorter than its diff:
```python
import math

import jax
import jax.numpy as jnp
from jax import lax
from jax.experimental import pallas as pl
from jax.experimental.pallas import tpu as pltpu
from jax.sharding import PartitionSpec as P

D = 5120
HD = 128
EPSILON = 1e-06
TOK = 384
WIDTH = 640
HEADS = WIDTH // HD
SLAB = 80
MASKED = -1e30
COLUMNS = ((0, 256), (256, 256), (512, 128))
NT = (((1,), (1,)), ((), ()))


def dot_nt(a, b):
    return lax.dot_general(a, b, NT, preferred_element_type=jnp.float32)


def dot_nn(a, b):
    return jnp.dot(a, b, preferred_element_type=jnp.float32)


def kernel(
    q_ref,
    k_ref,
    v_ref,
    table_ref,
    gate_ref,
    latent_ref,
    slab_ref,
    out_ref,
    squares,
    q_n,
    k_all,
    v_all,
    peak,
    total,
    mixed,
    gathered,
    weight,
    acc,
    staged,
    landed,
    gate_prev,
    sq_send,
    sq_recv,
    halo_send,
    halo_recv,
    gate_send,
    gate_recv,
    swap_send,
    swap_recv,
    side_send,
    side_recv,
    ring_send,
    ring_recv,
    twin_send,
    twin_recv,
    a_send,
    a_recv,
    f_send,
    f_recv,
    o_send,
    o_recv,
):
    sec = lax.axis_index("section")
    ten = lax.axis_index("tensor")
    z = lax.div(sec, 4)
    zh = lax.div(sec, 16)
    core = lax.rem(sec, 2)
    yl = lax.rem(lax.div(sec, 2), 2)
    x = lax.div(ten, 2)
    h = lax.rem(ten, 2)
    near = sec + 1 - 2 * core
    far = lax.rem(sec + 2 * core + 63, 64)
    following = lax.rem(sec + 1, 64)
    previous = lax.rem(sec + 63, 64)
    z_next = lax.rem(sec + 4, 64)
    z_last = lax.rem(sec + 60, 64)
    y_side = sec + 2 - 4 * yl
    x_right = lax.rem(x + 1, 4) * 2 + h
    x_left = lax.rem(x + 3, 4) * 2 + h
    other = ten + 1 - 2 * h
    swap_sec = 16 * x + lax.rem(sec, 16)
    swap_ten = 2 * zh + h
    stays = x == zh

    def remote(src, dst, send, recv, section, tensor):
        return pltpu.make_async_remote_copy(
            src_ref=src,
            dst_ref=dst,
            send_sem=send,
            recv_sem=recv,
            device_id={"section": section, "tensor": tensor},
            device_id_type=pl.DeviceIdType.MESH,
        )

    sent = []

    def send(src, dst, send_sem, recv_sem, section, tensor):
        copy = remote(src, dst, send_sem, recv_sem, section, tensor)
        copy.start()
        sent.append(copy)

    def arrived(dst, send_sem, recv_sem):
        remote(dst, dst, send_sem, recv_sem, near, ten).wait_recv()

    barrier = pltpu.get_barrier_semaphore()
    greeted = [(near, ten), (far, ten), (z_next, ten), (z_last, ten), (y_side, ten)]
    greeted += [(following, ten), (following, other), (previous, ten), (previous, other)]
    greeted += [(sec, lax.rem(ten + i, 8)) for i in range(1, 8)]
    for section, tensor in greeted:
        pl.semaphore_signal(
            barrier,
            inc=1,
            device_id={"section": section, "tensor": tensor},
            device_id_type=pl.DeviceIdType.MESH,
        )

    @pl.when(jnp.logical_not(stays))
    def _():
        pl.semaphore_signal(
            barrier,
            inc=1,
            device_id={"section": swap_sec, "tensor": swap_ten},
            device_id_type=pl.DeviceIdType.MESH,
        )

    def lanes(head):
        return slice(head * HD, (head + 1) * HD)

    def row_sums(ref):
        part = jnp.zeros((TOK, HD), jnp.float32)
        for head in range(HEADS):
            wide = ref[:, lanes(head)].astype(jnp.float32)
            part += wide * wide
        return jnp.sum(part.T, axis=0, keepdims=True)

    q_sums, k_sums = row_sums(q_ref), row_sums(k_ref)
    row = lax.broadcasted_iota(jnp.int32, (8, TOK), 0)
    squares[ten] = jnp.where(row < 4, q_sums, k_sums)

    pl.semaphore_wait(barrier, len(greeted) + jnp.where(stays, 0, 1))

    for i in range(1, 8):
        send(
            squares.at[ten], squares.at[ten], sq_send.at[i - 1], sq_recv.at[i - 1], sec,
            lax.rem(ten + i, 8),
        )

    def slab(zz, j, c):
        place = 4 * lax.rem(zz + 16, 16) + 2 * ((1 - yl) if j else yl) + c
        return weight.at[pl.ds(pl.multiple_of(place * SLAB, 16), SLAB)]

    swap = remote(
        slab_ref,
        weight.at[pl.ds(pl.multiple_of(swap_sec * SLAB, 16), SLAB)],
        swap_send,
        swap_recv,
        swap_sec,
        swap_ten,
    )
    keep = pltpu.make_async_copy(slab_ref, slab(z, 0, core), swap_send)

    @pl.when(jnp.logical_not(stays))
    def _():
        swap.start()

    @pl.when(stays)
    def _():
        keep.start()

    mine, by_near, by_far = (pl.ds(i * TOK, TOK) for i in range(3))
    v_near, v_far = v_all.at[pl.ds(0, TOK)], v_all.at[pl.ds(TOK, TOK)]
    send(v_ref, v_far, halo_send.at[0], halo_recv.at[0], far, ten)
    send(v_ref, v_near, halo_send.at[1], halo_recv.at[1], near, ten)
    send(gate_ref, gate_prev, gate_send, gate_recv, following, ten)

    def number(k, j):
        return 14 if k == 8 else 2 * (k - 1) + j

    def origin(d, k):
        return z + k if d else z - k

    def ring(d, k, j):
        n = number(k, j)
        piece = slab(origin(d, k - 1), j, core)
        send(piece, piece, ring_send.at[d, n], ring_recv.at[d, n], z_last if d else z_next, ten)

    def twin(piece, m):
        send(piece, piece, twin_send.at[m], twin_recv.at[m], near, ten)

    def first(j):
        piece = slab(z, j, core)
        for d in range(2):
            ring(d, 1, j)
        twin(piece, j)

    def pump(k):
        for j in range(2):
            for d in range(2):
                if k == 8 and j != d:
                    continue
                n = number(k, j)
                piece = slab(origin(d, k), j, core)
                arrived(piece, ring_send.at[d, n], ring_recv.at[d, n])
                if k < 7 or (k == 7 and j == d):
                    ring(d, k + 1, j)
                twin(piece, 2 + 15 * d + n)

    def twin_arrived(k):
        if k == 0:
            for j in range(2):
                arrived(slab(z, j, 1 - core), twin_send.at[j], twin_recv.at[j])
            return
        for j in range(2):
            for d in range(2):
                if k == 8 and j != d:
                    continue
                m = 2 + 15 * d + number(k, j)
                arrived(slab(origin(d, k), j, 1 - core), twin_send.at[m], twin_recv.at[m])

    @pl.when(jnp.logical_not(stays))
    def _():
        swap.wait_send()
        arrived(slab(z, 0, core), swap_send, swap_recv)

    @pl.when(stays)
    def _():
        keep.wait()

    own_slab = slab(z, 0, core)
    first(0)
    send(own_slab, own_slab, side_send, side_recv, y_side, ten)

    for i in range(1, 8):
        arrived(squares.at[lax.rem(ten + 8 - i, 8)], sq_send.at[i - 1], sq_recv.at[i - 1])
    sums = squares[0]
    for i in range(1, 8):
        sums = sums + squares[i]
    scale = lax.rsqrt(sums / D + EPSILON)
    q_scale = jnp.broadcast_to(scale[0:1], (HD, TOK)).T
    k_scale = jnp.broadcast_to(scale[4:5], (HD, TOK)).T

    def rotated(ref, head, at, by):
        wide = ref[:, lanes(head)].astype(jnp.float32)
        turned = wide * table_ref[at : at + 1, lanes(head)] + pltpu.roll(wide, HD // 2, 1) * (
            table_ref[at + 1 : at + 2, lanes(head)]
        )
        return (turned * by).astype(jnp.bfloat16)

    for head in range(HEADS):
        k_all[mine, lanes(head)] = rotated(k_ref, head, 2, k_scale)
    send(k_all.at[mine], k_all.at[by_far], halo_send.at[2], halo_recv.at[2], far, ten)
    send(k_all.at[mine], k_all.at[by_near], halo_send.at[3], halo_recv.at[3], near, ten)
    for head in range(HEADS):
        q_n[:, lanes(head)] = rotated(q_ref, head, 0, q_scale)

    arrived(slab(z, 1, core), side_send, side_recv)
    first(1)
    pump(1)

    arrived(v_near, halo_send.at[1], halo_recv.at[1])
    arrived(k_all.at[by_near], halo_send.at[3], halo_recv.at[3])
    for head in range(HEADS):
        scores = dot_nt(q_n[:, lanes(head)], k_all[0 : 2 * TOK, lanes(head)])
        highest = jnp.max(scores, axis=-1, keepdims=True)
        raised = jnp.exp2(scores - highest)
        peak[head] = jnp.broadcast_to(highest, (TOK, HD))
        total[head] = jnp.broadcast_to(jnp.sum(raised, axis=-1, keepdims=True), (TOK, HD))
        raised = raised.astype(jnp.bfloat16)
        mixed[head] = dot_nn(raised[:, :TOK], v_ref[:, lanes(head)]) + dot_nn(
            raised[:, TOK:], v_all[0:TOK, lanes(head)]
        )

    pump(2)
    pump(3)

    arrived(v_far, halo_send.at[0], halo_recv.at[0])
    arrived(k_all.at[by_far], halo_send.at[2], halo_recv.at[2])
    absent = jnp.where((sec == 0) | (sec == 63), MASKED, 0.0)

    def pass_on(head):
        for d in range(2):
            source = lax.rem(x + (1 if d else 3), 4)
            here = gathered.at[source, :, lanes(head)]
            arrived(here, a_send.at[d, head], a_recv.at[d, head])
            half = gathered.at[source, pl.ds(d * (TOK // 2), TOK // 2), lanes(head)]
            send(half, half, f_send.at[d, head], f_recv.at[d, head], sec, x_left if d else x_right)

    for head in range(HEADS):
        scores = dot_nt(q_n[:, lanes(head)], k_all[2 * TOK :, lanes(head)]) + absent
        before = peak[head]
        highest = jnp.maximum(before[:, 0:1], jnp.max(scores, axis=-1, keepdims=True))
        raised = jnp.exp2(scores - highest)
        shrink = jnp.exp2(before - highest)
        sums = total[head] * shrink + jnp.sum(raised, axis=-1, keepdims=True)
        result = mixed[head] * shrink + dot_nn(
            raised.astype(jnp.bfloat16), v_all[TOK : 2 * TOK, lanes(head)]
        )
        gathered[x, :, lanes(head)] = (result / sums).astype(jnp.bfloat16)
        own = gathered.at[x, :, lanes(head)]
        for d in range(2):
            send(own, own, a_send.at[d, head], a_recv.at[d, head], sec, x_left if d else x_right)
        if head >= 2:
            pass_on(head - 2)
    pump(4)
    pass_on(HEADS - 2)
    pass_on(HEADS - 1)
    pump(5)
    pump(6)
    pump(7)

    def columns_of(block, half, start, size):
        return weight[pl.ds(pl.multiple_of(block * 1280 + half * WIDTH + start, 16), size)]

    for k in range(8):
        twin_arrived(k)
    for head in range(HEADS):
        for d in range(2):
            half = gathered.at[
                lax.rem(x + 2, 4), pl.ds(d * (TOK // 2), TOK // 2), lanes(head)
            ]
            arrived(half, f_send.at[d, head], f_recv.at[d, head])
    halves = (1 - h, h)
    for step, shift in enumerate((0, 1, 3)):
        block = lax.rem(zh + shift, 4)
        for i, half in enumerate(halves):
            term = dot_nt(gathered[block], columns_of(block, half, 0, WIDTH))
            acc[i] = term if step == 0 else acc[i] + term
    pump(8)
    twin_arrived(8)
    block = lax.rem(zh + 2, 4)
    for i, half in enumerate(halves):
        for c, (start, size) in enumerate(COLUMNS):
            where = slice(start, start + size)
            term = acc[i, :, where] + dot_nt(
                gathered[block], columns_of(block, half, start, size)
            )
            if i == 1:
                term = latent_ref[:, where].astype(jnp.float32) + gate_ref[0:1, where] * term
            staged[i, :, where] = term.astype(jnp.bfloat16)
            send(
                staged.at[i, :, where],
                landed.at[i, :, where],
                o_send.at[i, c],
                o_recv.at[i, c],
                following,
                ten if i else other,
            )

    arrived(gate_prev, gate_send, gate_recv)
    for c, (start, size) in enumerate(COLUMNS):
        where = slice(start, start + size)
        for i in range(2):
            arrived(landed.at[i, :, where], o_send.at[i, c], o_recv.at[i, c])
        out_ref[:, where] = (
            landed[1, :, where].astype(jnp.float32)
            + gate_prev[0:1, where] * landed[0, :, where].astype(jnp.float32)
        ).astype(jnp.bfloat16)

    for copy in sent:
        copy.wait_send()


def body(
    queries,
    keys,
    values,
    q_gain,
    k_gain,
    frame_offset,
    noise_level,
    gate_table,
    out_weight,
    latent,
    fresh,
):
    half_width = HD // 2
    pair_rate = jnp.exp(
        jnp.arange(half_width, dtype=jnp.float32) * (-math.log(10000.0) / half_width)
    )
    angles = frame_offset[0].astype(jnp.float32) * pair_rate
    cosines, sines = jnp.cos(angles), jnp.sin(angles)
    straight = jnp.concatenate([cosines, cosines])
    crossed = jnp.concatenate([-sines, sines])

    def tables(gain, factor):
        by_head = gain.reshape(HEADS, HD) * factor
        swapped = jnp.concatenate([by_head[:, half_width:], by_head[:, :half_width]], axis=1)
        return [(by_head * straight).reshape(-1), (swapped * crossed).reshape(-1)]

    table = jnp.stack(
        tables(q_gain, math.log2(math.e) / math.sqrt(HD)) + tables(k_gain, 1.0)
        + [jnp.zeros((WIDTH,), jnp.float32)] * 4
    )
    gate_row = lax.dynamic_index_in_dim(gate_table, noise_level[0], 0, keepdims=True)
    gate = jnp.broadcast_to(gate_row, (8, WIDTH))

    bf16, f32 = jnp.bfloat16, jnp.float32
    dma = pltpu.SemaphoreType.DMA
    moved = pl.pallas_call(
        kernel,
        out_shape=jax.ShapeDtypeStruct((TOK, WIDTH), bf16),
        in_specs=[pl.BlockSpec(memory_space=pltpu.VMEM)] * 7,
        out_specs=pl.BlockSpec(memory_space=pltpu.VMEM),
        scratch_shapes=[
            pltpu.VMEM((8, 8, TOK), f32),
            pltpu.VMEM((TOK, WIDTH), bf16),
            pltpu.VMEM((3 * TOK, WIDTH), bf16),
            pltpu.VMEM((2 * TOK, WIDTH), bf16),
            pltpu.VMEM((HEADS, TOK, HD), f32),
            pltpu.VMEM((HEADS, TOK, HD), f32),
            pltpu.VMEM((HEADS, TOK, HD), f32),
            pltpu.VMEM((4, TOK, WIDTH), bf16),
            pltpu.VMEM((D, WIDTH), bf16),
            pltpu.VMEM((2, TOK, WIDTH), f32),
            pltpu.VMEM((2, TOK, WIDTH), bf16),
            pltpu.VMEM((2, TOK, WIDTH), bf16),
            pltpu.VMEM((8, WIDTH), f32),
            dma((7,)),
            dma((7,)),
            dma((4,)),
            dma((4,)),
            dma,
            dma,
            dma,
            dma,
            dma,
            dma,
            dma((2, 15)),
            dma((2, 15)),
            dma((32,)),
            dma((32,)),
            dma((2, HEADS)),
            dma((2, HEADS)),
            dma((2, HEADS)),
            dma((2, HEADS)),
            dma((2, len(COLUMNS))),
            dma((2, len(COLUMNS))),
        ],
        compiler_params=pltpu.CompilerParams(
            collective_id=0, has_side_effects=True, vmem_limit_bytes=48 * 1024 * 1024
        ),
        cost_estimate=pl.CostEstimate(
            flops=3_700_000_000, bytes_accessed=4_000_000, transcendentals=2_300_000
        ),
    )(queries, keys, values, table, gate, latent, out_weight.T)
    return jnp.where(lax.axis_index("section") == 0, fresh, moved)


def solution(mesh):
    in_specs = (
        P("section", "tensor"),
        P("section", "tensor"),
        P("section", "tensor"),
        P("tensor"),
        P("tensor"),
        P("section"),
        P("section"),
        P(None, "tensor"),
        P("tensor", "section"),
        P("section", "tensor"),
        P(None, "tensor"),
    )
    out_specs = P("section", "tensor")
    return jax.shard_map(body, mesh=mesh, in_specs=in_specs, out_specs=out_specs, check_vma=False)
```

time: 275 us -> 113 us (0.41)
  the two profiles are of different devices: /device:TPU:128 before, /device:TPU:32 now
where the time goes in v1:
time: 113 us; the launch traced here: 112 us
  Pallas kernels  104 us (92%)
  local copies, waits for them, and re-layouts  5.37 us (5%)
  between operations  1.48 us (1%)
  other arithmetic  1.19 us (1%)
    pallas_call x1, Pallas kernels, body(): pl.pallas_call(kernel, out_shape=jax.ShapeDtypeStruct((TOK, WIDTH), bf16)...  104 us
    unnamed x20, local copies, waits for them, and re-layouts  5.16 us

profile of v1, /device:TPU:32, one launch (start us, length us, event | category | flops | bytes accessed | tf_op | source)
XLA Modules:
  0.0 112.5 jit_solution(380281292609171175)
XLA Ops:
  0.0 0.0 copy-start
  0.7 0.0 copy-start.8
  0.8 0.1 pad_maximum_fusion
  0.8 0.5 copy-done.8
  1.4 0.0 copy-start.7
  1.4 0.1 fusion.6
  1.5 0.0 copy-start.5
  1.5 0.1 pad_maximum_fusion.1
  1.6 0.5 copy-done.7
  2.1 0.1 fusion.5
  2.2 0.1 fusion.1
  3.0 0.0 copy-done
  3.0 0.0 copy-done.5
  3.0 0.0 copy-start.1
  3.0 1.0 copy-done.1
  4.1 0.0 copy-start.2
  4.1 1.0 copy-done.2
  5.1 0.0 copy-start.3
  5.1 1.0 copy-done.3
  6.1 0.0 copy-start.4
  6.1 1.0 copy-done.4
  7.2 0.0 copy-start.6
  7.2 104.4 %shard_map.109 = bf16[384,640]{1,0:T(8,128)(2,1)S(1)} custom-call(bf16[384,640]{1,0:T(8,128)(2,1)S(1)} %copy-done.1, bf16[384,640]{1,0:T(8,128)(2,1)S(1)} %copy-done.2, bf16[384,640]{1,0:T(8,128)(2,1)S(1)} %copy-done.3, f32[8,640]{1,0:T(8,128)S(1)} %stack.7.table_ref, f32[8,640]{1,0:T(8,128)S(1)} %broadcast_in_dim.5.gate_ref, ...), custom_call_target="tpu_custom_call" | custom-call | flops 3700000000 | bytes 4000000 | tf_op jit(solution)/shard_map/pallas_call | solution.py:409
  111.6 0.0 copy-done.6
  111.6 0.8 broadcast_select_fusion
  (12 shorter events, 0.2 us)
Async XLA Ops:
  0.0 3.0 %copy-start = (f32[128,640]{1,0:T(8,128)S(1)}, f32[128,640]{1,0:T(8,128)}, u32[]{:S(2)}) copy-start(f32[128,640]{1,0:T(8,128)} %param.18) | copy-start | bytes 983044
  0.7 0.7 copy-start.8
  1.4 0.7 copy-start.7
  1.5 1.6 %copy-start.5 = (bf16[640,80]{0,1:T(8,128)(2,1)S(1)}, bf16[640,80]{0,1:T(8,128)(2,1)}, u32[]{:S(2)}) copy-start(bf16[640,80]{0,1:T(8,128)(2,1)} %param.19) | copy-start | bytes 307204
  3.0 1.0 copy-start.1
  4.1 1.0 copy-start.2
  5.1 1.0 copy-start.3
  6.1 1.0 copy-start.4
  7.2 104.4 %copy-start.6 = (bf16[384,640]{1,0:T(8,128)(2,1)S(1)}, bf16[384,640]{1,0:T(8,128)(2,1)}, u32[]{:S(2)}) copy-start(bf16[384,640]{1,0:T(8,128)(2,1)} %param.21) | copy-start | bytes 1474564

commit v2 on v1

--- a/solution.py
+++ b/solution.py
@@ -15,7 +15,7 @@
 HEADS = WIDTH // HD
 SLAB = 80
 MASKED = -1e30
-COLUMNS = ((0, 256), (256, 256), (512, 128))
+PIECES = ((0, 2), (2, 1), (3, 2))
 NT = (((1,), (1,)), ((), ()))
 
 
@@ -28,14 +28,23 @@
 
 
 def kernel(
+    offset_ref,
+    level_ref,
+    gain_ref,
+    q_hbm,
+    k_hbm,
+    v_hbm,
+    gate_hbm,
+    latent_hbm,
+    slab_ref,
+    out_ref,
     q_ref,
     k_ref,
     v_ref,
-    table_ref,
+    gate_table,
+    latent_ref,
     gate_ref,
-    latent_ref,
-    slab_ref,
-    out_ref,
+    load_sem,
     squares,
     q_n,
     k_all,
@@ -45,7 +54,6 @@
     mixed,
     gathered,
     weight,
-    acc,
     staged,
     landed,
     gate_prev,
@@ -102,6 +110,23 @@
             device_id_type=pl.DeviceIdType.MESH,
         )
 
+    loads = [
+        pltpu.make_async_copy(src, dst, load_sem.at[i])
+        for i, (src, dst) in enumerate(
+            (
+                (k_hbm, k_ref),
+                (q_hbm, q_ref),
+                (v_hbm, v_ref),
+                (gate_hbm, gate_table),
+            )
+            + tuple(
+                (latent_hbm.at[:, pl.ds(t * HD, HD)], latent_ref.at[t]) for t in range(HEADS)
+            )
+        )
+    ]
+    for load in loads:
+        load.start()
+
     sent = []
 
     def send(src, dst, send_sem, recv_sem, section, tensor):
@@ -143,7 +168,18 @@
             part += wide * wide
         return jnp.sum(part.T, axis=0, keepdims=True)
 
-    q_sums, k_sums = row_sums(q_ref), row_sums(k_ref)
+    lane = lax.broadcasted_iota(jnp.int32, (1, HD), 1)
+    pair = lax.rem(lane, HD // 2).astype(jnp.float32)
+    angles = offset_ref[0].astype(jnp.float32) * jnp.exp(
+        pair * (-math.log(10000.0) / (HD // 2))
+    )
+    straight = jnp.cos(angles)
+    crossed = jnp.where(lane < HD // 2, -1.0, 1.0) * jnp.sin(angles)
+
+    loads[0].wait()
+    k_sums = row_sums(k_ref)
+    loads[1].wait()
+    q_sums = row_sums(q_ref)
     row = lax.broadcasted_iota(jnp.int32, (8, TOK), 0)
     squares[ten] = jnp.where(row < 4, q_sums, k_sums)
 
@@ -179,9 +215,8 @@
 
     mine, by_near, by_far = (pl.ds(i * TOK, TOK) for i in range(3))
     v_near, v_far = v_all.at[pl.ds(0, TOK)], v_all.at[pl.ds(TOK, TOK)]
-    send(v_ref, v_far, halo_send.at[0], halo_recv.at[0], far, ten)
-    send(v_ref, v_near, halo_send.at[1], halo_recv.at[1], near, ten)
-    send(gate_ref, gate_prev, gate_send, gate_recv, following, ten)
+    send(v_hbm, v_far, halo_send.at[0], halo_recv.at[0], far, ten)
+    send(v_hbm, v_near, halo_send.at[1], halo_recv.at[1], near, ten)
 
     def number(k, j):
         return 14 if k == 8 else 2 * (k - 1) + j
@@ -192,28 +227,82 @@
     def ring(d, k, j):
         n = number(k, j)
         piece = slab(origin(d, k - 1), j, core)
-        send(piece, piece, ring_send.at[d, n], ring_recv.at[d, n], z_last if d else z_next, ten)
-
-    def twin(piece, m):
-        send(piece, piece, twin_send.at[m], twin_recv.at[m], near, ten)
+        return remote(
+            piece, piece, ring_send.at[d, n], ring_recv.at[d, n], z_last if d else z_next, ten
+        )
+
+    def across(d, k):
+        piece = slab(origin(d, k), 0, core)
+        d, n = (1 if k == 8 else d), number(k, 1)
+        return remote(piece, piece, ring_send.at[d, n], ring_recv.at[d, n], y_side, ten)
+
+    def twin_copy(piece, m):
+        return remote(piece, piece, twin_send.at[m], twin_recv.at[m], near, ten)
+
+    def directions(k, j):
+        return (j,) if k == 8 else (0, 1)
+
+    even, odd = core == 0, core == 1
 
     def first(j):
-        piece = slab(z, j, core)
         for d in range(2):
-            ring(d, 1, j)
-        twin(piece, j)
+            if j == 0:
+                ring(d, 1, 0).start()
+            else:
+
+                @pl.when(odd)
+                def _(d=d):
+                    ring(d, 1, 1).start()
+
+        twin_copy(slab(z, j, core), j).start()
+
+    def second_column(k, forward):
+        for d in directions(k, 1):
+            n = number(k, 1)
+            piece = slab(origin(d, k), 1, core)
+            arrived(piece, ring_send.at[d, n], ring_recv.at[d, n])
+            if forward and (k < 7 or (k == 7 and d == 1)):
+                ring(d, k + 1, 1).start()
+            twin_copy(piece, 2 + 15 * d + n).start()
 
     def pump(k):
-        for j in range(2):
-            for d in range(2):
-                if k == 8 and j != d:
-                    continue
-                n = number(k, j)
-                piece = slab(origin(d, k), j, core)
-                arrived(piece, ring_send.at[d, n], ring_recv.at[d, n])
-                if k < 7 or (k == 7 and j == d):
-                    ring(d, k + 1, j)
-                twin(piece, 2 + 15 * d + n)
+        for d in directions(k, 0):
+            n = number(k, 0)
+            piece = slab(origin(d, k), 0, core)
+            arrived(piece, ring_send.at[d, n], ring_recv.at[d, n])
+            if k < 7 or (k == 7 and d == 0):
+                ring(d, k + 1, 0).start()
+
+            @pl.when(even)
+            def _(d=d):
+                across(d, k).start()
+
+            twin_copy(piece, 2 + 15 * d + n).start()
+
+        @pl.when(odd)
+        def _():
+            second_column(k, True)
+
+        if 1 < k < 8:
+            second_of_even(k - 1)
+
+    def second_of_even(k):
+        @pl.when(even)
+        def _():
+            second_column(k, False)
+
+    def ring_sent():
+        for m in range(2):
+            twin_copy(slab(z, m, core), m).wait_send()
+        for k in range(1, 9):
+            for j in range(2):
+                for d in directions(k, j):
+                    n = number(k, j)
+                    remote(
+                        slab(z, 0, core), slab(z, 0, core), ring_send.at[d, n],
+                        ring_recv.at[d, n], near, ten,
+                    ).wait_send()
+                    twin_copy(slab(origin(d, k), j, core), 2 + 15 * d + n).wait_send()
 
     def twin_arrived(k):
         if k == 0:
@@ -227,46 +316,31 @@
                 m = 2 + 15 * d + number(k, j)
                 arrived(slab(origin(d, k), j, 1 - core), twin_send.at[m], twin_recv.at[m])
 
-    @pl.when(jnp.logical_not(stays))
-    def _():
-        swap.wait_send()
-        arrived(slab(z, 0, core), swap_send, swap_recv)
-
-    @pl.when(stays)
-    def _():
-        keep.wait()
-
-    own_slab = slab(z, 0, core)
-    first(0)
-    send(own_slab, own_slab, side_send, side_recv, y_side, ten)
-
     for i in range(1, 8):
         arrived(squares.at[lax.rem(ten + 8 - i, 8)], sq_send.at[i - 1], sq_recv.at[i - 1])
     sums = squares[0]
     for i in range(1, 8):
         sums = sums + squares[i]
     scale = lax.rsqrt(sums / D + EPSILON)
-    q_scale = jnp.broadcast_to(scale[0:1], (HD, TOK)).T
+    q_scale = jnp.broadcast_to(scale[0:1] * (math.log2(math.e) / math.sqrt(HD)), (HD, TOK)).T
     k_scale = jnp.broadcast_to(scale[4:5], (HD, TOK)).T
 
     def rotated(ref, head, at, by):
         wide = ref[:, lanes(head)].astype(jnp.float32)
-        turned = wide * table_ref[at : at + 1, lanes(head)] + pltpu.roll(wide, HD // 2, 1) * (
-            table_ref[at + 1 : at + 2, lanes(head)]
+        gain = gain_ref[at : at + 1, lanes(head)]
+        turned = wide * (gain * straight) + pltpu.roll(wide, HD // 2, 1) * (
+            pltpu.roll(gain, HD // 2, 1) * crossed
         )
         return (turned * by).astype(jnp.bfloat16)
 
     for head in range(HEADS):
-        k_all[mine, lanes(head)] = rotated(k_ref, head, 2, k_scale)
+        k_all[mine, lanes(head)] = rotated(k_ref, head, 1, k_scale)
     send(k_all.at[mine], k_all.at[by_far], halo_send.at[2], halo_recv.at[2], far, ten)
     send(k_all.at[mine], k_all.at[by_near], halo_send.at[3], halo_recv.at[3], near, ten)
     for head in range(HEADS):
         q_n[:, lanes(head)] = rotated(q_ref, head, 0, q_scale)
 
-    arrived(slab(z, 1, core), side_send, side_recv)
-    first(1)
-    pump(1)
-
+    loads[2].wait()
     arrived(v_near, halo_send.at[1], halo_recv.at[1])
     arrived(k_all.at[by_near], halo_send.at[3], halo_recv.at[3])
     for head in range(HEADS):
@@ -280,8 +354,32 @@
             raised[:, TOK:], v_all[0:TOK, lanes(head)]
         )
 
+    @pl.when(jnp.logical_not(stays))
+    def _():
+        swap.wait_send()
+        arrived(slab(z, 0, core), swap_send, swap_recv)
+
+    @pl.when(stays)
+    def _():
+        keep.wait()
+
+    own_slab = slab(z, 0, core)
+    first(0)
+    send(own_slab, own_slab, side_send, side_recv, y_side, ten)
+
+    loads[3].wait()
+    gate_row = gate_table[pl.ds(level_ref[0], 1), :]
+    for t in range(HEADS):
+        gate_ref[t] = jnp.broadcast_to(gate_row[:, lanes(t)], (8, HD))
+    send(gate_ref, gate_prev, gate_send, gate_recv, following, ten)
+    for load in loads[4:]:
+        load.wait()
+    arrived(slab(z, 1, core), side_send, side_recv)
+    first(1)
+    pump(1)
     pump(2)
     pump(3)
+    pump(4)
 
     arrived(v_far, halo_send.at[0], halo_recv.at[0])
     arrived(k_all.at[by_far], halo_send.at[2], halo_recv.at[2])
@@ -309,65 +407,78 @@
         own = gathered.at[x, :, lanes(head)]
         for d in range(2):
             send(own, own, a_send.at[d, head], a_recv.at[d, head], sec, x_left if d else x_right)
-        if head >= 2:
-            pass_on(head - 2)
-    pump(4)
-    pass_on(HEADS - 2)
-    pass_on(HEADS - 1)
-    pump(5)
+        if head == 2:
+            pump(5)
+            pass_on(0)
+    pass_on(1)
+    pass_on(2)
     pump(6)
+    pass_on(3)
+    pass_on(4)
     pump(7)
 
-    def columns_of(block, half, start, size):
-        return weight[pl.ds(pl.multiple_of(block * 1280 + half * WIDTH + start, 16), size)]
-
-    for k in range(8):
+    def project(half, piece, first_tile, tiles):
+        own = half == h
+        i = jnp.where(own, 1, 0)
+        value = jnp.zeros((TOK, tiles * HD), jnp.float32)
+        for block in range(4):
+            start = block * 1280 + half * WIDTH + first_tile * HD
+            value += dot_nt(
+                gathered[block], weight[pl.ds(pl.multiple_of(start, HD), tiles * HD), :]
+            )
+        for t in range(tiles):
+            part = value[:, lanes(t)]
+            updated = (
+                latent_ref[first_tile + t].astype(jnp.float32) + gate_ref[first_tile + t][0:1] * part
+            )
+            staged[i, first_tile + t] = jnp.where(own, updated, part).astype(jnp.bfloat16)
+        send(
+            staged.at[i, pl.ds(first_tile, tiles)],
+            landed.at[i, pl.ds(first_tile, tiles)],
+            o_send.at[i, piece],
+            o_recv.at[i, piece],
+            following,
+            jnp.where(own, ten, other),
+        )
+
+    def project_side(shift):
+        column = lax.rem(z + shift, 4)
+        side = lax.rem(column, 2)
+        project(lax.div(column, 2), 2 * side, 3 * side, 2)
+
+    def project_middle(shift):
+        project(lax.div(lax.rem(z + shift, 4), 2), 1, 2, 1)
+
+    for k in range(7):
         twin_arrived(k)
     for head in range(HEADS):
         for d in range(2):
-            half = gathered.at[
-                lax.rem(x + 2, 4), pl.ds(d * (TOK // 2), TOK // 2), lanes(head)
-            ]
+            half = gathered.at[lax.rem(x + 2, 4), pl.ds(d * (TOK // 2), TOK // 2), lanes(head)]
             arrived(half, f_send.at[d, head], f_recv.at[d, head])
-    halves = (1 - h, h)
-    for step, shift in enumerate((0, 1, 3)):
-        block = lax.rem(zh + shift, 4)
-        for i, half in enumerate(halves):
-            term = dot_nt(gathered[block], columns_of(block, half, 0, WIDTH))
-            acc[i] = term if step == 0 else acc[i] + term
+    project_side(2)
+    second_of_even(7)
+    twin_arrived(7)
+    project_side(1)
     pump(8)
+    project_side(3)
+    project_middle(2)
+    second_of_even(8)
     twin_arrived(8)
-    block = lax.rem(zh + 2, 4)
-    for i, half in enumerate(halves):
-        for c, (start, size) in enumerate(COLUMNS):
-            where = slice(start, start + size)
-            term = acc[i, :, where] + dot_nt(
-                gathered[block], columns_of(block, half, start, size)
-            )
-            if i == 1:
-                term = latent_ref[:, where].astype(jnp.float32) + gate_ref[0:1, where] * term
-            staged[i, :, where] = term.astype(jnp.bfloat16)
-            send(
-                staged.at[i, :, where],
-                landed.at[i, :, where],
-                o_send.at[i, c],
-                o_recv.at[i, c],
-                following,
-                ten if i else other,
-            )
-
-    arrived(gate_prev, gate_send, gate_recv)
-    for c, (start, size) in enumerate(COLUMNS):
-        where = slice(start, start + size)
-        for i in range(2):
-            arrived(landed.at[i, :, where], o_send.at[i, c], o_recv.at[i, c])
-        out_ref[:, where] = (
-            landed[1, :, where].astype(jnp.float32)
-            + gate_prev[0:1, where] * landed[0, :, where].astype(jnp.float32)
-        ).astype(jnp.bfloat16)
-
+    project_side(0)
+    project_middle(0)
+
+    ring_sent()
     for copy in sent:
         copy.wait_send()
+    arrived(gate_prev, gate_send, gate_recv)
+    for c, (start, size) in enumerate(PIECES):
+        for i in range(2):
+            arrived(landed.at[i, pl.ds(start, size)], o_send.at[i, c], o_recv.at[i, c])
+        for t in range(start, start + size):
+            out_ref[:, lanes(t)] = (
+                landed[1, t].astype(jnp.float32)
+                + gate_prev[t][0:1] * landed[0, t].astype(jnp.float32)
+            ).astype(jnp.bfloat16)
 
 
 def body(
@@ -383,35 +494,24 @@
     latent,
     fresh,
 ):
-    half_width = HD // 2
-    pair_rate = jnp.exp(
-        jnp.arange(half_width, dtype=jnp.float32) * (-math.log(10000.0) / half_width)
-    )
-    angles = frame_offset[0].astype(jnp.float32) * pair_rate
-    cosines, sines = jnp.cos(angles), jnp.sin(angles)
-    straight = jnp.concatenate([cosines, cosines])
-    crossed = jnp.concatenate([-sines, sines])
-
-    def tables(gain, factor):
-        by_head = gain.reshape(HEADS, HD) * factor
-        swapped = jnp.concatenate([by_head[:, half_width:], by_head[:, :half_width]], axis=1)
-        return [(by_head * straight).reshape(-1), (swapped * crossed).reshape(-1)]
-
-    table = jnp.stack(
-        tables(q_gain, math.log2(math.e) / math.sqrt(HD)) + tables(k_gain, 1.0)
-        + [jnp.zeros((WIDTH,), jnp.float32)] * 4
-    )
-    gate_row = lax.dynamic_index_in_dim(gate_table, noise_level[0], 0, keepdims=True)
-    gate = jnp.broadcast_to(gate_row, (8, WIDTH))
-
+    gains = jnp.stack([q_gain, k_gain])
     bf16, f32 = jnp.bfloat16, jnp.float32
     dma = pltpu.SemaphoreType.DMA
     moved = pl.pallas_call(
         kernel,
         out_shape=jax.ShapeDtypeStruct((TOK, WIDTH), bf16),
-        in_specs=[pl.BlockSpec(memory_space=pltpu.VMEM)] * 7,
+        in_specs=[pl.BlockSpec(memory_space=pltpu.SMEM)] * 2
+        + [pl.BlockSpec(memory_space=pltpu.VMEM)]
+        + [pl.BlockSpec(memory_space=pltpu.HBM)] * 6,
         out_specs=pl.BlockSpec(memory_space=pltpu.VMEM),
         scratch_shapes=[
+            pltpu.VMEM((TOK, WIDTH), bf16),
+            pltpu.VMEM((TOK, WIDTH), bf16),
+            pltpu.VMEM((TOK, WIDTH), bf16),
+            pltpu.VMEM((128, WIDTH), f32),
+            pltpu.VMEM((HEADS, TOK, HD), bf16),
+            pltpu.VMEM((HEADS, 8, HD), f32),
+            dma((4 + HEADS,)),
             pltpu.VMEM((8, 8, TOK), f32),
             pltpu.VMEM((TOK, WIDTH), bf16),
             pltpu.VMEM((3 * TOK, WIDTH), bf16),
@@ -421,10 +521,9 @@
             pltpu.VMEM((HEADS, TOK, HD), f32),
             pltpu.VMEM((4, TOK, WIDTH), bf16),
             pltpu.VMEM((D, WIDTH), bf16),
-            pltpu.VMEM((2, TOK, WIDTH), f32),
-            pltpu.VMEM((2, TOK, WIDTH), bf16),
-            pltpu.VMEM((2, TOK, WIDTH), bf16),
-            pltpu.VMEM((8, WIDTH), f32),
+            pltpu.VMEM((2, HEADS, TOK, HD), bf16),
+            pltpu.VMEM((2, HEADS, TOK, HD), bf16),
+            pltpu.VMEM((HEADS, 8, HD), f32),
             dma((7,)),
             dma((7,)),
             dma((4,)),
@@ -443,16 +542,18 @@
             dma((2, HEADS)),
             dma((2, HEADS)),
             dma((2, HEADS)),
-            dma((2, len(COLUMNS))),
-            dma((2, len(COLUMNS))),
+            dma((2, len(PIECES))),
+            dma((2, len(PIECES))),
         ],
         compiler_params=pltpu.CompilerParams(
-            collective_id=0, has_side_effects=True, vmem_limit_bytes=48 * 1024 * 1024
+            collective_id=0, has_side_effects=True, vmem_limit_bytes=60 * 1024 * 1024
         ),
         cost_estimate=pl.CostEstimate(
             flops=3_700_000_000, bytes_accessed=4_000_000, transcendentals=2_300_000
         ),
-    )(queries, keys, values, table, gate, latent, out_weight.T)
+    )(
+        frame_offset, noise_level, gains, queries, keys, values, gate_table, latent, out_weight.T
+    )
     return jnp.where(lax.axis_index("section") == 0, fresh, moved)
 
 

time: 113 us -> 105 us (0.929)
  the two profiles are of different devices: /device:TPU:32 before, /device:TPU:9 now
where the time goes in v2:
time: 105 us
  Pallas kernels  101 us (96%)
  other arithmetic  2.48 us (2%)
  between operations  1.33 us (1%)
    pallas_call x1, Pallas kernels, body(): pl.pallas_call(kernel, out_shape=jax.ShapeDtypeStruct((TOK, WIDTH), bf16)...  101 us

profile of v2, /device:TPU:9, one launch (start us, length us, event | category | flops | bytes accessed | tf_op | source)
XLA Modules:
  0.0 105.2 jit_solution(16204154974848352454)
XLA Ops:
  0.0 0.0 copy-start.1
  0.0 0.7 stack.10
  0.7 0.0 copy-done.1
  0.7 0.6 pad_maximum_fusion.gain_ref
  2.6 0.0 copy-start
  2.6 100.7 %shard_map.109 = bf16[384,640]{1,0:T(8,128)(2,1)} custom-call(s32[1]{0:T(128)S(6)} %copy.12.offset_ref, s32[1]{0:T(128)S(6)} %copy.13.level_ref, f32[2,640]{1,0:T(2,128)} %pad_maximum_fusion.gain_ref, bf16[384,640]{1,0:T(8,128)(2,1)} %q_hbm.1, bf16[384,640]{1,0:T(8,128)(2,1)} %k_hbm.1, bf16[384,640]{1,0:T(8,128)(2,1)} %v_hbm.1, f32[128,640]{1,0:T(8,128)} %gate_hbm.1, ...), custom_call_target="tpu_custom_call" | custom-call | flops 3700000000 | bytes 4000000 | tf_op jit(solution)/shard_map/pallas_call | solution.py:500
  103.3 0.0 copy-done
  103.3 1.9 %broadcast_select_fusion = bf16[384,640]{1,0:T(8,128)(2,1)} fusion(bf16[384,640]{1,0:T(8,128)(2,1)S(1)} %copy-done, bf16[384,640]{1,0:T(8,128)(2,1)} %shard_map.109, pred[]{:T(512)S(6)} %eq.3), kind=kLoop, calls=%fused_computation | loop fusion | flops 245760 | bytes 1474561 | tf_op jit(solution)/shard_map/jit(_where)/select_n | solution.py:557
  (1 shorter events, 0.0 us)
Async XLA Ops:
  0.0 0.7 copy-start.1
  2.6 100.7 %copy-start = (bf16[384,640]{1,0:T(8,128)(2,1)S(1)}, bf16[384,640]{1,0:T(8,128)(2,1)}, u32[]{:S(2)}) copy-start(bf16[384,640]{1,0:T(8,128)(2,1)} %param.21) | copy-start | bytes 1474564

commit v3 on v2

--- a/solution.py
+++ b/solution.py
@@ -15,6 +15,8 @@
 HEADS = WIDTH // HD
 SLAB = 80
 MASKED = -1e30
+PARTS = ((0, 48), (48, 32))
+LAG = 3
 PIECES = ((0, 2), (2, 1), (3, 2))
 NT = (((1,), (1,)), ((), ()))
 
@@ -215,7 +217,11 @@
 
     mine, by_near, by_far = (pl.ds(i * TOK, TOK) for i in range(3))
     v_near, v_far = v_all.at[pl.ds(0, TOK)], v_all.at[pl.ds(TOK, TOK)]
-    send(v_hbm, v_far, halo_send.at[0], halo_recv.at[0], far, ten)
+    for head in range(HEADS):
+        send(
+            v_hbm.at[:, lanes(head)], v_far.at[:, lanes(head)], halo_send.at[9 + head],
+            halo_recv.at[9 + head], far, ten,
+        )
     send(v_hbm, v_near, halo_send.at[1], halo_recv.at[1], near, ten)
 
     def number(k, j):
@@ -224,17 +230,22 @@
     def origin(d, k):
         return z + k if d else z - k
 
-    def ring(d, k, j):
+    def part_of(zz, j, p):
+        start, size = PARTS[p]
+        place = 4 * lax.rem(zz + 16, 16) + 2 * ((1 - yl) if j else yl) + core
+        return weight.at[pl.ds(pl.multiple_of(place * SLAB + start, 16), size)]
+
+    def ring(d, k, j, p):
         n = number(k, j)
-        piece = slab(origin(d, k - 1), j, core)
+        piece = part_of(origin(d, k - 1), j, p)
         return remote(
-            piece, piece, ring_send.at[d, n], ring_recv.at[d, n], z_last if d else z_next, ten
+            piece, piece, ring_send.at[d, n, p], ring_recv.at[d, n, p], z_last if d else z_next, ten
         )
 
     def across(d, k):
         piece = slab(origin(d, k), 0, core)
         d, n = (1 if k == 8 else d), number(k, 1)
-        return remote(piece, piece, ring_send.at[d, n], ring_recv.at[d, n], y_side, ten)
+        return remote(piece, piece, ring_send.at[d, n, 0], ring_recv.at[d, n, 0], y_side, ten)
 
     def twin_copy(piece, m):
         return remote(piece, piece, twin_send.at[m], twin_recv.at[m], near, ten)
@@ -244,52 +255,54 @@
 
     even, odd = core == 0, core == 1
 
+    parts = range(len(PARTS))
+
     def first(j):
-        for d in range(2):
-            if j == 0:
-                ring(d, 1, 0).start()
-            else:
-
-                @pl.when(odd)
-                def _(d=d):
-                    ring(d, 1, 1).start()
-
+        def start():
+            for p in parts:
+                for d in range(2):
+                    ring(d, 1, j, p).start()
+
+        if j == 0:
+            start()
+        else:
+            pl.when(odd)(start)
         twin_copy(slab(z, j, core), j).start()
 
-    def second_column(k, forward):
-        for d in directions(k, 1):
-            n = number(k, 1)
-            piece = slab(origin(d, k), 1, core)
-            arrived(piece, ring_send.at[d, n], ring_recv.at[d, n])
-            if forward and (k < 7 or (k == 7 and d == 1)):
-                ring(d, k + 1, 1).start()
-            twin_copy(piece, 2 + 15 * d + n).start()
+    def pass_slab(k, j):
+        n = number(k, j)
+        for p in parts:
+            for d in directions(k, j):
+                arrived(part_of(origin(d, k), j, p), ring_send.at[d, n, p], ring_recv.at[d, n, p])
+                if k < 7 or (k == 7 and d == j):
+                    ring(d, k + 1, j, p).start()
+                if p == len(PARTS) - 1:
+                    if j == 0:
+
+                        @pl.when(even)
+                        def _(d=d):
+                            across(d, k).start()
+
+                    twin_copy(slab(origin(d, k), j, core), 2 + 15 * d + n).start()
 
     def pump(k):
-        for d in directions(k, 0):
-            n = number(k, 0)
-            piece = slab(origin(d, k), 0, core)
-            arrived(piece, ring_send.at[d, n], ring_recv.at[d, n])
-            if k < 7 or (k == 7 and d == 0):
-                ring(d, k + 1, 0).start()
-
-            @pl.when(even)
-            def _(d=d):
-                across(d, k).start()
-
-            twin_copy(piece, 2 + 15 * d + n).start()
+        pass_slab(k, 0)
 
         @pl.when(odd)
         def _():
-            second_column(k, True)
-
-        if 1 < k < 8:
-            second_of_even(k - 1)
+            pass_slab(k, 1)
+
+        if LAG < k < 8:
+            second_of_even(k - LAG)
 
     def second_of_even(k):
         @pl.when(even)
         def _():
-            second_column(k, False)
+            n = number(k, 1)
+            for d in directions(k, 1):
+                piece = slab(origin(d, k), 1, core)
+                arrived(piece, ring_send.at[d, n, 0], ring_recv.at[d, n, 0])
+                twin_copy(piece, 2 + 15 * d + n).start()
 
     def ring_sent():
         for m in range(2):
@@ -297,12 +310,23 @@
         for k in range(1, 9):
             for j in range(2):
                 for d in directions(k, j):
-                    n = number(k, j)
-                    remote(
-                        slab(z, 0, core), slab(z, 0, core), ring_send.at[d, n],
-                        ring_recv.at[d, n], near, ten,
-                    ).wait_send()
-                    twin_copy(slab(origin(d, k), j, core), 2 + 15 * d + n).wait_send()
+                    twin_copy(slab(origin(d, k), j, core), 2 + 15 * d + number(k, j)).wait_send()
+                    if j == 0:
+                        for p in parts:
+                            ring(d, k, 0, p).wait_send()
+
+        @pl.when(odd)
+        def _():
+            for k in range(1, 9):
+                for d in directions(k, 1):
+                    for p in parts:
+                        ring(d, k, 1, p).wait_send()
+
+        @pl.when(even)
+        def _():
+            for k in range(1, 9):
+                for d in directions(k, 0):
+                    across(d, k).wait_send()
 
     def twin_arrived(k):
         if k == 0:
@@ -335,10 +359,36 @@
 
     for head in range(HEADS):
         k_all[mine, lanes(head)] = rotated(k_ref, head, 1, k_scale)
-    send(k_all.at[mine], k_all.at[by_far], halo_send.at[2], halo_recv.at[2], far, ten)
+        send(
+            k_all.at[mine, lanes(head)], k_all.at[by_far, lanes(head)], halo_send.at[4 + head],
+            halo_recv.at[4 + head], far, ten,
+        )
     send(k_all.at[mine], k_all.at[by_near], halo_send.at[3], halo_recv.at[3], near, ten)
     for head in range(HEADS):
         q_n[:, lanes(head)] = rotated(q_ref, head, 0, q_scale)
+
+    @pl.when(jnp.logical_not(stays))
+    def _():
+        swap.wait_send()
+        arrived(slab(z, 0, core), swap_send, swap_recv)
+
+    @pl.when(stays)
+    def _():
+        keep.wait()
+
+    own_slab = slab(z, 0, core)
+    first(0)
+    send(own_slab, own_slab, side_send, side_recv, y_side, ten)
+
+    loads[3].wait()
+    gate_row = gate_table[pl.ds(level_ref[0], 1), :]
+    for t in range(HEADS):
+        gate_ref[t] = jnp.broadcast_to(gate_row[:, lanes(t)], (8, HD))
+    send(gate_ref, gate_prev, gate_send, gate_recv, following, ten)
+    for load in loads[4:]:
+        load.wait()
+    arrived(slab(z, 1, core), side_send, side_recv)
+    first(1)
 
     loads[2].wait()
     arrived(v_near, halo_send.at[1], halo_recv.at[1])
@@ -354,35 +404,9 @@
             raised[:, TOK:], v_all[0:TOK, lanes(head)]
         )
 
-    @pl.when(jnp.logical_not(stays))
-    def _():
-        swap.wait_send()
-        arrived(slab(z, 0, core), swap_send, swap_recv)
-
-    @pl.when(stays)
-    def _():
-        keep.wait()
-
-    own_slab = slab(z, 0, core)
-    first(0)
-    send(own_slab, own_slab, side_send, side_recv, y_side, ten)
-
-    loads[3].wait()
-    gate_row = gate_table[pl.ds(level_ref[0], 1), :]
-    for t in range(HEADS):
-        gate_ref[t] = jnp.broadcast_to(gate_row[:, lanes(t)], (8, HD))
-    send(gate_ref, gate_prev, gate_send, gate_recv, following, ten)
-    for load in loads[4:]:
-        load.wait()
-    arrived(slab(z, 1, core), side_send, side_recv)
-    first(1)
     pump(1)
     pump(2)
-    pump(3)
-    pump(4)
-
-    arrived(v_far, halo_send.at[0], halo_recv.at[0])
-    arrived(k_all.at[by_far], halo_send.at[2], halo_recv.at[2])
+
     absent = jnp.where((sec == 0) | (sec == 63), MASKED, 0.0)
 
     def pass_on(head):
@@ -394,6 +418,12 @@
             send(half, half, f_send.at[d, head], f_recv.at[d, head], sec, x_left if d else x_right)
 
     for head in range(HEADS):
+        arrived(
+            k_all.at[by_far, lanes(head)], halo_send.at[4 + head], halo_recv.at[4 + head]
+        )
+        arrived(
+            v_far.at[:, lanes(head)], halo_send.at[9 + head], halo_recv.at[9 + head]
+        )
         scores = dot_nt(q_n[:, lanes(head)], k_all[2 * TOK :, lanes(head)]) + absent
         before = peak[head]
         highest = jnp.maximum(before[:, 0:1], jnp.max(scores, axis=-1, keepdims=True))
@@ -407,11 +437,14 @@
         own = gathered.at[x, :, lanes(head)]
         for d in range(2):
             send(own, own, a_send.at[d, head], a_recv.at[d, head], sec, x_left if d else x_right)
-        if head == 2:
-            pump(5)
+        if head == 1:
+            pump(3)
             pass_on(0)
-    pass_on(1)
+        if head == 3:
+            pump(4)
+            pass_on(1)
     pass_on(2)
+    pump(5)
     pump(6)
     pass_on(3)
     pass_on(4)
@@ -449,6 +482,8 @@
     def project_middle(shift):
         project(lax.div(lax.rem(z + shift, 4), 2), 1, 2, 1)
 
+    second_of_even(5)
+    second_of_even(6)
     for k in range(7):
         twin_arrived(k)
     for head in range(HEADS):
@@ -456,10 +491,10 @@
             half = gathered.at[lax.rem(x + 2, 4), pl.ds(d * (TOK // 2), TOK // 2), lanes(head)]
             arrived(half, f_send.at[d, head], f_recv.at[d, head])
     project_side(2)
+    pump(8)
     second_of_even(7)
     twin_arrived(7)
     project_side(1)
-    pump(8)
     project_side(3)
     project_middle(2)
     second_of_even(8)
@@ -526,16 +561,16 @@
             pltpu.VMEM((HEADS, 8, HD), f32),
             dma((7,)),
             dma((7,)),
-            dma((4,)),
-            dma((4,)),
+            dma((14,)),
+            dma((14,)),
             dma,
             dma,
             dma,
             dma,
             dma,
             dma,
-            dma((2, 15)),
-            dma((2, 15)),
+            dma((2, 15, len(PARTS))),
+            dma((2, 15, len(PARTS))),
             dma((32,)),
             dma((32,)),
             dma((2, HEADS)),

time: 105 us -> 100 us (0.952)
  Pallas kernels: 101 us -> 95.5 us
    pallas_call x1, Pallas kernels: 101 us -> 95.5 us  [body(): pl.pallas_call(kernel, out_shape=jax.ShapeDtypeStruct((TOK, WIDTH), bf16)...]
where the time goes in v3:
time: 100 us
  Pallas kernels  95.5 us (96%)
  other arithmetic  2.48 us (2%)
  between operations  1.33 us (1%)
    pallas_call x1, Pallas kernels, body(): pl.pallas_call(kernel, out_shape=jax.ShapeDtypeStruct((TOK, WIDTH), bf16)...  95.5 us

profile of v3, /device:TPU:9, one launch (start us, length us, event | category | flops | bytes accessed | tf_op | source)
XLA Modules:
  0.0 100.0 jit_solution(14321759839037523269)
XLA Ops:
  0.0 0.0 copy-start.1
  0.0 0.7 stack.10
  0.7 0.0 copy-done.1
  0.7 0.6 pad_maximum_fusion.gain_ref
  2.6 0.0 copy-start
  2.6 95.5 %shard_map.109 = bf16[384,640]{1,0:T(8,128)(2,1)} custom-call(s32[1]{0:T(128)S(6)} %copy.12.offset_ref, s32[1]{0:T(128)S(6)} %copy.13.level_ref, f32[2,640]{1,0:T(2,128)} %pad_maximum_fusion.gain_ref, bf16[384,640]{1,0:T(8,128)(2,1)} %q_hbm.1, bf16[384,640]{1,0:T(8,128)(2,1)} %k_hbm.1, bf16[384,640]{1,0:T(8,128)(2,1)} %v_hbm.1, f32[128,640]{1,0:T(8,128)} %gate_hbm.1, ...), custom_call_target="tpu_custom_call" | custom-call | flops 3700000000 | bytes 4000000 | tf_op jit(solution)/shard_map/pallas_call | solution.py:535
  98.1 0.0 copy-done
  98.1 1.9 %broadcast_select_fusion = bf16[384,640]{1,0:T(8,128)(2,1)} fusion(bf16[384,640]{1,0:T(8,128)(2,1)S(1)} %copy-done, bf16[384,640]{1,0:T(8,128)(2,1)} %shard_map.109, pred[]{:T(512)S(6)} %eq.3), kind=kLoop, calls=%fused_computation | loop fusion | flops 245760 | bytes 1474561 | tf_op jit(solution)/shard_map/jit(_where)/select_n | solution.py:592
  (1 shorter events, 0.0 us)
Async XLA Ops:
  0.0 0.7 copy-start.1
  2.6 95.5 %copy-start = (bf16[384,640]{1,0:T(8,128)(2,1)S(1)}, bf16[384,640]{1,0:T(8,128)(2,1)}, u32[]{:S(2)}) copy-start(bf16[384,640]{1,0:T(8,128)(2,1)} %param.21) | copy-start | bytes 1474564
